TPU v7x, 32 devices: a whole 2x2x4 slice. The times are simulated.
32 devices in a mesh: cuts: 4 (over x, core), tile: 8 (over z, y).
Axes of the slice: x: 2, y: 2, z: 4, core: 2. Of those that a mesh axis runs over, the one named last changes fastest.
Arguments:
- state_in: float32 [4, 2, 128, 1024], P('cuts', None, 'tile'), may hold values from -0.625 to 0.625
- sea_depth: float32 [128, 1024], P('tile'), may hold values from 1.5 to 3
- pressure: float32 [128, 1024], P('tile'), may hold values from -3 to 3
Outputs:
- state_out: float32 [4, 2, 128, 1024], P('cuts', None, 'tile')
All inputs are finite; a program needn't handle non-finite values.
Results may differ from a plain program's by a relative error of at most 0.0003.
Values sent between devices are 32-bit elements; how exact they have to be, the bound alone decides.
A program may use at most 64 MiB of HBM per device.

v0:
```python
import jax
import jax.numpy as jnp
from jax import lax
from jax.sharding import PartitionSpec as P

LEVELS = 8
DEFECT = 3


TIME_STEP = 0.8
SHIP_SPEED = 0.5
EPSILON = 1e-06


def padded_2(block, sides, width):
    for axis, dim in sides:
        count = lax.axis_size(axis)
        forward = [(i, i + 1) for i in range(count - 1)]
        backward = [(target, source) for source, target in forward]
        low = lax.ppermute(
            lax.slice_in_dim(block, block.shape[dim] - width, None, axis=dim), axis, forward
        )
        high = lax.ppermute(lax.slice_in_dim(block, 0, width, axis=dim), axis, backward)
        block = jnp.concatenate([low, block, high], axis=dim)
    return block


def shifted(block, axis, distance):
    devices = range(lax.axis_size(axis))
    route = [(i - distance, i) for i in devices if i - distance in devices]
    return lax.ppermute(block, axis, route)


def horizontal(padded):
    middle = padded[..., 1:-1, :]
    widened = jnp.pad(middle, [(0, 0)] * (middle.ndim - 1) + [(1, 1)])
    return (
        padded[..., 2:, :]
        + padded[..., :-2, :]
        + widened[..., 2:]
        + widened[..., :-2]
        - 4.0 * middle
    )


def vertical_part(potential, surface, vertical):
    above = jnp.concatenate([potential[1:], surface[None]], axis=0)
    below = jnp.concatenate([potential[1:2], potential[:-1]], axis=0)
    return vertical * (above - 2.0 * potential + below)


def operator(padded, surface, vertical):
    return horizontal(padded) + vertical_part(padded[:, 1:-1, :], surface, vertical)


def elimination(vertical):
    diagonal = -2.0 * vertical - 4.0
    inverses = [1.0 / diagonal]
    ratios = [2.0 * vertical * inverses[0]]
    for level in range(1, LEVELS):
        inverse = 1.0 / (diagonal - vertical * ratios[-1])
        inverses.append(inverse)
        ratios.append(vertical * inverse)
    return (inverses, ratios)


def tridiagonal(residual, vertical, factors):
    inverses, ratios = factors
    forward = [residual[0] * inverses[0]]
    for level in range(1, LEVELS):
        forward.append((residual[level] - vertical * forward[-1]) * inverses[level])
    solution = [forward[-1]]
    for level in range(LEVELS - 2, -1, -1):
        solution.append(forward[level] - ratios[level] * solution[-1])
    return jnp.stack(solution[::-1])


def global_products(residual, image):
    cross_sum, image_sum = lax.psum((jnp.sum(residual * image), jnp.sum(image * image)), "tile")
    return cross_sum / (image_sum + EPSILON)


def solve_narrow(state, vertical, factors):
    padded = padded_2(state, (("tile", 1),), 1)
    potential_top = state[1]
    potential = jnp.broadcast_to(potential_top, (LEVELS,) + potential_top.shape)
    spread = jnp.broadcast_to(padded[1], (LEVELS,) + padded[1].shape)
    residual = -operator(spread, potential_top, vertical)
    flat_zero = jnp.zeros_like(potential_top)
    for sweep in range(DEFECT):
        correction = tridiagonal(residual, vertical, factors)
        widened_corr = padded_2(correction, (("tile", 1),), 1)
        image = operator(widened_corr, flat_zero, vertical)
        step_size = global_products(residual, image)
        potential = potential + step_size * correction
        if sweep + 1 < DEFECT:
            residual = residual - step_size * image
    return (padded, potential)


def tendency(state, sea_depth, pressure, vertical, factors):
    elevation, potential_top = (state[0], state[1])
    padded, potential = solve_narrow(state, vertical, factors)
    vertical_vel = (
        (3.0 * potential_top - 4.0 * potential[-1] + potential[-2]) * LEVELS / (2.0 * sea_depth)
    )
    east = (padded[:, 2:, :] - padded[:, :-2, :]) * 0.5
    widened = jnp.pad(state, ((0, 0), (0, 0), (1, 1)))
    north = (widened[:, :, 2:] - widened[:, :, :-2]) * 0.5
    slope_sq = east[0] * east[0] + north[0] * north[0]
    height_rate = (
        SHIP_SPEED * east[0]
        - (east[0] * east[1] + north[0] * north[1])
        + vertical_vel * (1.0 + slope_sq)
    )
    flow_rate = (
        SHIP_SPEED * east[1]
        - elevation
        - 0.5 * (east[1] * east[1] + north[1] * north[1])
        + 0.5 * vertical_vel * vertical_vel * (1.0 + slope_sq)
        - pressure
    )
    return jnp.stack([height_rate, flow_rate])


def runge_kutta(state, sea_depth, pressure, vertical, factors):
    rate_one = tendency(state, sea_depth, pressure, vertical, factors)
    rate_two = tendency(state + 0.5 * TIME_STEP * rate_one, sea_depth, pressure, vertical, factors)
    rate_three = tendency(
        state + 0.5 * TIME_STEP * rate_two, sea_depth, pressure, vertical, factors
    )
    rate_four = tendency(state + TIME_STEP * rate_three, sea_depth, pressure, vertical, factors)
    return state + TIME_STEP / 6.0 * (rate_one + 2.0 * rate_two + 2.0 * rate_three + rate_four)


def coarse_matrix(sea_depth):
    stiffness = jnp.tanh(sea_depth)
    frequency = jnp.sqrt(stiffness)
    cosine = jnp.cos(TIME_STEP * frequency)
    sine_part = jnp.sin(TIME_STEP * frequency)
    return (cosine, stiffness * sine_part / frequency, -sine_part / frequency, cosine)


def coarse_apply(coarse, state):
    return jnp.stack(
        [coarse[0] * state[0] + coarse[1] * state[1], coarse[2] * state[0] + coarse[3] * state[1]]
    )


def local(state_in, sea_depth, pressure):
    start_state = state_in[0]
    vertical = (LEVELS / sea_depth) ** 2
    factors = elimination(vertical)
    fine_state = runge_kutta(start_state, sea_depth, pressure, vertical, factors)
    coarse = coarse_matrix(sea_depth)
    defect = fine_state - coarse_apply(coarse, start_state)
    first_result = coarse_apply(coarse, start_state) + defect
    position = lax.axis_index("cuts")
    is_first = position == 0

    def link(turn, current):
        arrived = shifted(current, "cuts", 1)
        begin = jnp.where(is_first, start_state, arrived)
        return coarse_apply(coarse, begin) + defect

    result = lax.fori_loop(0, lax.axis_size("cuts") - 1, link, first_result)
    return result[None]


def solution(mesh):
    placed = (P("cuts", None, "tile", None), P("tile", None), P("tile", None))
    return jax.shard_map(
        local, mesh=mesh, in_specs=placed, out_specs=P("cuts", None, "tile", None), check_vma=False
    )
```

profile of v0, /device:TPU:3, one launch (start us, length us, event | category | flops | bytes accessed | tf_op | source)
XLA Modules:
  0.0 446.6 jit_solution(10705841612309130390)
XLA Ops:
  2.2 4.1 collective-permute-start.2
  10.1 4.7 %collective-permute-start.4 = (f32[8,1,1024]{2,1,0:T(1,128)S(1)}, f32[8,1,1024]{2,1,0:T(1,128)S(1)}, u32[]{:S(2)}, u32[]{:S(2)}) collective-permute-start(f32[8,1,1024]{2,1,0:T(1,128)S(1)} %get-tuple-element.301), channel_id=1, source_target_pairs={{0,1},{1,2},{2,3},{3,4},{4,5},{5,6},{6,7},{8,9},{9,10},{10,11},{11... | collective-permute-start | bytes 98312 | tf_op jit(solution)/shard_map/ppermute | solution.py:20
  17.2 20.5 %all-reduce.43 = (f32[]{:T(128)}, f32[]{:T(128)}) all-reduce(f32[]{:T(128)} %get-tuple-element.71, f32[]{:T(128)} %get-tuple-element.70), channel_id=1, replica_groups=mesh['cuts'=4,'tile'=8] {'tile'}, use_global_device_ids=true, to_apply=%region_1.2 | all-reduce | flops 2 | bytes 16 | tf_op jit(solution)/shard_map/psum | solution.py:79
  41.2 4.0 collective-permute-start.6
  48.4 16.4 %all-reduce.42 = (f32[]{:T(128)}, f32[]{:T(128)}) all-reduce(f32[]{:T(128)} %get-tuple-element.69, f32[]{:T(128)} %get-tuple-element.68), channel_id=1, replica_groups=mesh['cuts'=4,'tile'=8] {'tile'}, use_global_device_ids=true, to_apply=%region_5.6 | all-reduce | flops 2 | bytes 16 | tf_op jit(solution)/shard_map/psum | solution.py:79
  69.4 4.0 collective-permute-start.8
  75.5 16.1 %all-reduce.41 = (f32[]{:T(128)}, f32[]{:T(128)}) all-reduce(f32[]{:T(128)} %get-tuple-element.67, f32[]{:T(128)} %get-tuple-element.66), channel_id=1, replica_groups=mesh['cuts'=4,'tile'=8] {'tile'}, use_global_device_ids=true, to_apply=%region_9.10 | all-reduce | flops 2 | bytes 16 | tf_op jit(solution)/shard_map/psum | solution.py:79
  109.6 16.3 %all-reduce.40 = (f32[]{:T(128)}, f32[]{:T(128)}) all-reduce(f32[]{:T(128)} %get-tuple-element.65, f32[]{:T(128)} %get-tuple-element.64), channel_id=1, replica_groups=mesh['cuts'=4,'tile'=8] {'tile'}, use_global_device_ids=true, to_apply=%region_13.14 | all-reduce | flops 2 | bytes 16 | tf_op jit(solution)/shard_map/psum | solution.py:79
  136.5 16.2 %all-reduce.39 = (f32[]{:T(128)}, f32[]{:T(128)}) all-reduce(f32[]{:T(128)} %get-tuple-element.63, f32[]{:T(128)} %get-tuple-element.62), channel_id=1, replica_groups=mesh['cuts'=4,'tile'=8] {'tile'}, use_global_device_ids=true, to_apply=%region_17.18 | all-reduce | flops 2 | bytes 16 | tf_op jit(solution)/shard_map/psum | solution.py:79
  157.3 4.2 collective-permute-start.16
  163.4 16.0 %all-reduce.38 = (f32[]{:T(128)}, f32[]{:T(128)}) all-reduce(f32[]{:T(128)} %get-tuple-element.61, f32[]{:T(128)} %get-tuple-element.60), channel_id=1, replica_groups=mesh['cuts'=4,'tile'=8] {'tile'}, use_global_device_ids=true, to_apply=%region_21.22 | all-reduce | flops 2 | bytes 16 | tf_op jit(solution)/shard_map/psum | solution.py:79
  190.5 4.2 collective-permute-start.20
  197.3 16.6 %all-reduce.37 = (f32[]{:T(128)}, f32[]{:T(128)}) all-reduce(f32[]{:T(128)} %get-tuple-element.59, f32[]{:T(128)} %get-tuple-element.58), channel_id=1, replica_groups=mesh['cuts'=4,'tile'=8] {'tile'}, use_global_device_ids=true, to_apply=%region_25.26 | all-reduce | flops 2 | bytes 16 | tf_op jit(solution)/shard_map/psum | solution.py:79
  224.8 16.1 %all-reduce.36 = (f32[]{:T(128)}, f32[]{:T(128)}) all-reduce(f32[]{:T(128)} %get-tuple-element.57, f32[]{:T(128)} %get-tuple-element.56), channel_id=1, replica_groups=mesh['cuts'=4,'tile'=8] {'tile'}, use_global_device_ids=true, to_apply=%region_29.30 | all-reduce | flops 2 | bytes 16 | tf_op jit(solution)/shard_map/psum | solution.py:79
  251.6 16.0 %all-reduce.35 = (f32[]{:T(128)}, f32[]{:T(128)}) all-reduce(f32[]{:T(128)} %get-tuple-element.55, f32[]{:T(128)} %get-tuple-element.54), channel_id=1, replica_groups=mesh['cuts'=4,'tile'=8] {'tile'}, use_global_device_ids=true, to_apply=%region_33.34 | all-reduce | flops 2 | bytes 16 | tf_op jit(solution)/shard_map/psum | solution.py:79
  279.4 4.2 collective-permute-start.28
  286.2 16.6 %all-reduce.34 = (f32[]{:T(128)}, f32[]{:T(128)}) all-reduce(f32[]{:T(128)} %get-tuple-element.53, f32[]{:T(128)} %get-tuple-element.52), channel_id=1, replica_groups=mesh['cuts'=4,'tile'=8] {'tile'}, use_global_device_ids=true, to_apply=%region_37.38 | all-reduce | flops 2 | bytes 16 | tf_op jit(solution)/shard_map/psum | solution.py:79
  308.3 4.6 %collective-permute-start.30 = (f32[8,1,1024]{2,1,0:T(1,128)}, f32[8,1,1024]{2,1,0:T(1,128)}, u32[]{:S(2)}, u32[]{:S(2)}) collective-permute-start(f32[8,1,1024]{2,1,0:T(1,128)} %get-tuple-element.281), channel_id=1, source_target_pairs={{0,1},{1,2},{2,3},{3,4},{4,5},{5,6},{6,7},{8,9},{9,10},{10,11},{11... | collective-permute-start | bytes 98312 | tf_op jit(solution)/shard_map/ppermute | solution.py:20
  317.0 16.0 %all-reduce.33 = (f32[]{:T(128)}, f32[]{:T(128)}) all-reduce(f32[]{:T(128)} %get-tuple-element.51, f32[]{:T(128)} %get-tuple-element.50), channel_id=1, replica_groups=mesh['cuts'=4,'tile'=8] {'tile'}, use_global_device_ids=true, to_apply=%region_41.42 | all-reduce | flops 2 | bytes 16 | tf_op jit(solution)/shard_map/psum | solution.py:79
  343.6 16.1 %all-reduce.32 = (f32[]{:T(128)}, f32[]{:T(128)}) all-reduce(f32[]{:T(128)} %get-tuple-element.49, f32[]{:T(128)} %get-tuple-element.48), channel_id=1, replica_groups=mesh['cuts'=4,'tile'=8] {'tile'}, use_global_device_ids=true, to_apply=%region_45.46 | all-reduce | flops 2 | bytes 16 | tf_op jit(solution)/shard_map/psum | solution.py:79
  363.1 82.9 %while.10 = (s32[]{:T(128)}, f32[2,16,1024]{2,1,0:T(8,128)S(1)}, f32[16,1024]{1,0:T(8,128)S(1)}, pred[]{:T(512)}, f32[2,16,1024]{2,1,0:T(8,128)S(1)}, /*index=5*...) while((s32[]{:T(128)}, f32[2,16,1024]{2,1,0:T(8,128)S(1)}, ...), condition=%wide.region_49.50_spmd, body=%wide.region_48.49_spmd.sunk | while | flops 196610 | bytes 1769606 | solution.py:166
  364.4 68.7 %collective-permute-done = f32[2,16,1024]{2,1,0:T(8,128)S(1)} collective-permute-done((f32[2,16,1024]{2,1,0:T(8,128)S(1)}, f32[2,16,1024]{2,1,0:T(8,128)S(1)}, u32[]{:S(2)}, u32[]{:S(2)}) %collective-permute-start) | collective-permute-done | bytes 131104 | tf_op jit(solution)/shard_map/while/body/eval_jaxpr/ppermute | solution.py:31
  434.5 5.0 %collective-permute-done = f32[2,16,1024]{2,1,0:T(8,128)S(1)} collective-permute-done((f32[2,16,1024]{2,1,0:T(8,128)S(1)}, f32[2,16,1024]{2,1,0:T(8,128)S(1)}, u32[]{:S(2)}, u32[]{:S(2)}) %collective-permute-start) | collective-permute-done | bytes 131104 | tf_op jit(solution)/shard_map/while/body/eval_jaxpr/ppermute | solution.py:31
  440.9 5.0 %collective-permute-done = f32[2,16,1024]{2,1,0:T(8,128)S(1)} collective-permute-done((f32[2,16,1024]{2,1,0:T(8,128)S(1)}, f32[2,16,1024]{2,1,0:T(8,128)S(1)}, u32[]{:S(2)}, u32[]{:S(2)}) %collective-permute-start) | collective-permute-done | bytes 131104 | tf_op jit(solution)/shard_map/while/body/eval_jaxpr/ppermute | solution.py:31
  (329 shorter events, 118.0 us)
Async XLA Ops:
  0.9 6.4 %collective-permute-start.1 = (f32[2,1,1024]{2,1,0:T(1,128)S(1)}, f32[2,1,1024]{2,1,0:T(1,128)S(1)}, u32[]{:S(2)}, u32[]{:S(2)}) collective-permute-start(f32[2,1,1024]{2,1,0:T(1,128)S(1)} %get-tuple-element.337), channel_id=1, source_target_pairs={{1,0},{2,1},{3,2},{4,3},{5,4},{6,5},{7,6},{9,8},{10,9},{11,10},{12... | collective-permute-start | bytes 24584 | tf_op jit(solution)/shard_map/ppermute | solution.py:23
  2.2 5.1 %collective-permute-start.2 = (f32[2,1,1024]{2,1,0:T(1,128)S(1)}, f32[2,1,1024]{2,1,0:T(1,128)S(1)}, u32[]{:S(2)}, u32[]{:S(2)}) collective-permute-start(f32[2,1,1024]{2,1,0:T(1,128)S(1)} %get-tuple-element.338), channel_id=1, source_target_pairs={{0,1},{1,2},{2,3},{3,4},{4,5},{5,6},{6,7},{8,9},{9,10},{10,11},{11... | collective-permute-start | bytes 24584 | tf_op jit(solution)/shard_map/ppermute | solution.py:20
  8.8 6.0 %collective-permute-start.3 = (f32[8,1,1024]{2,1,0:T(1,128)S(1)}, f32[8,1,1024]{2,1,0:T(1,128)S(1)}, u32[]{:S(2)}, u32[]{:S(2)}) collective-permute-start(f32[8,1,1024]{2,1,0:T(1,128)S(1)} %get-tuple-element.300), channel_id=1, source_target_pairs={{1,0},{2,1},{3,2},{4,3},{5,4},{6,5},{7,6},{9,8},{10,9},{11,10},{12... | collective-permute-start | bytes 98312 | tf_op jit(solution)/shard_map/ppermute | solution.py:23
  10.1 5.7 %collective-permute-start.4 = (f32[8,1,1024]{2,1,0:T(1,128)S(1)}, f32[8,1,1024]{2,1,0:T(1,128)S(1)}, u32[]{:S(2)}, u32[]{:S(2)}) collective-permute-start(f32[8,1,1024]{2,1,0:T(1,128)S(1)} %get-tuple-element.301), channel_id=1, source_target_pairs={{0,1},{1,2},{2,3},{3,4},{4,5},{5,6},{6,7},{8,9},{9,10},{10,11},{11... | collective-permute-start | bytes 98312 | tf_op jit(solution)/shard_map/ppermute | solution.py:20
  39.9 5.3 %collective-permute-start.5 = (f32[8,1,1024]{2,1,0:T(1,128)S(1)}, f32[8,1,1024]{2,1,0:T(1,128)S(1)}, u32[]{:S(2)}, u32[]{:S(2)}) collective-permute-start(f32[8,1,1024]{2,1,0:T(1,128)S(1)} %get-tuple-element.298), channel_id=1, source_target_pairs={{1,0},{2,1},{3,2},{4,3},{5,4},{6,5},{7,6},{9,8},{10,9},{11,10},{12... | collective-permute-start | bytes 98312 | tf_op jit(solution)/shard_map/ppermute | solution.py:23
  68.1 5.4 %collective-permute-start.7 = (f32[8,1,1024]{2,1,0:T(1,128)S(1)}, f32[8,1,1024]{2,1,0:T(1,128)S(1)}, u32[]{:S(2)}, u32[]{:S(2)}) collective-permute-start(f32[8,1,1024]{2,1,0:T(1,128)S(1)} %get-tuple-element.296), channel_id=1, source_target_pairs={{1,0},{2,1},{3,2},{4,3},{5,4},{6,5},{7,6},{9,8},{10,9},{11,10},{12... | collective-permute-start | bytes 98312 | tf_op jit(solution)/shard_map/ppermute | solution.py:23
  69.4 5.0 %collective-permute-start.8 = (f32[8,1,1024]{2,1,0:T(1,128)S(1)}, f32[8,1,1024]{2,1,0:T(1,128)S(1)}, u32[]{:S(2)}, u32[]{:S(2)}) collective-permute-start(f32[8,1,1024]{2,1,0:T(1,128)S(1)} %get-tuple-element.297), channel_id=1, source_target_pairs={{0,1},{1,2},{2,3},{3,4},{4,5},{5,6},{6,7},{8,9},{9,10},{10,11},{11... | collective-permute-start | bytes 98312 | tf_op jit(solution)/shard_map/ppermute | solution.py:20
  101.8 5.3 %collective-permute-start.11 = (f32[8,1,1024]{2,1,0:T(1,128)S(1)}, f32[8,1,1024]{2,1,0:T(1,128)S(1)}, u32[]{:S(2)}, u32[]{:S(2)}) collective-permute-start(f32[8,1,1024]{2,1,0:T(1,128)S(1)} %get-tuple-element.294), channel_id=1, source_target_pairs={{1,0},{2,1},{3,2},{4,3},{5,4},{6,5},{7,6},{9,8},{10,9},{11,10},{12... | collective-permute-start | bytes 98312 | tf_op jit(solution)/shard_map/ppermute | solution.py:23
  128.0 5.3 %collective-permute-start.13 = (f32[8,1,1024]{2,1,0:T(1,128)S(1)}, f32[8,1,1024]{2,1,0:T(1,128)S(1)}, u32[]{:S(2)}, u32[]{:S(2)}) collective-permute-start(f32[8,1,1024]{2,1,0:T(1,128)S(1)} %get-tuple-element.292), channel_id=1, source_target_pairs={{1,0},{2,1},{3,2},{4,3},{5,4},{6,5},{7,6},{9,8},{10,9},{11,10},{12... | collective-permute-start | bytes 98312 | tf_op jit(solution)/shard_map/ppermute | solution.py:23
  156.0 5.6 %collective-permute-start.15 = (f32[8,1,1024]{2,1,0:T(1,128)S(1)}, f32[8,1,1024]{2,1,0:T(1,128)S(1)}, u32[]{:S(2)}, u32[]{:S(2)}) collective-permute-start(f32[8,1,1024]{2,1,0:T(1,128)S(1)} %get-tuple-element.290), channel_id=1, source_target_pairs={{1,0},{2,1},{3,2},{4,3},{5,4},{6,5},{7,6},{9,8},{10,9},{11,10},{12... | collective-permute-start | bytes 98312 | tf_op jit(solution)/shard_map/ppermute | solution.py:23
  181.6 5.3 %collective-permute-start.17 = (f32[2,1,1024]{2,1,0:T(1,128)S(1)}, f32[2,1,1024]{2,1,0:T(1,128)S(1)}, u32[]{:S(2)}, u32[]{:S(2)}) collective-permute-start(f32[2,1,1024]{2,1,0:T(1,128)S(1)} %get-tuple-element.320), channel_id=1, source_target_pairs={{1,0},{2,1},{3,2},{4,3},{5,4},{6,5},{7,6},{9,8},{10,9},{11,10},{12... | collective-permute-start | bytes 24584 | tf_op jit(solution)/shard_map/ppermute | solution.py:23
  189.2 5.6 %collective-permute-start.19 = (f32[8,1,1024]{2,1,0:T(1,128)S(1)}, f32[8,1,1024]{2,1,0:T(1,128)S(1)}, u32[]{:S(2)}, u32[]{:S(2)}) collective-permute-start(f32[8,1,1024]{2,1,0:T(1,128)S(1)} %get-tuple-element.288), channel_id=1, source_target_pairs={{1,0},{2,1},{3,2},{4,3},{5,4},{6,5},{7,6},{9,8},{10,9},{11,10},{12... | collective-permute-start | bytes 98312 | tf_op jit(solution)/shard_map/ppermute | solution.py:23
  190.5 5.3 %collective-permute-start.20 = (f32[8,1,1024]{2,1,0:T(1,128)S(1)}, f32[8,1,1024]{2,1,0:T(1,128)S(1)}, u32[]{:S(2)}, u32[]{:S(2)}) collective-permute-start(f32[8,1,1024]{2,1,0:T(1,128)S(1)} %get-tuple-element.289), channel_id=1, source_target_pairs={{0,1},{1,2},{2,3},{3,4},{4,5},{5,6},{6,7},{8,9},{9,10},{10,11},{11... | collective-permute-start | bytes 98312 | tf_op jit(solution)/shard_map/ppermute | solution.py:20
  216.2 5.3 %collective-permute-start.21 = (f32[8,1,1024]{2,1,0:T(1,128)S(1)}, f32[8,1,1024]{2,1,0:T(1,128)S(1)}, u32[]{:S(2)}, u32[]{:S(2)}) collective-permute-start(f32[8,1,1024]{2,1,0:T(1,128)S(1)} %get-tuple-element.286), channel_id=1, source_target_pairs={{1,0},{2,1},{3,2},{4,3},{5,4},{6,5},{7,6},{9,8},{10,9},{11,10},{12... | collective-permute-start | bytes 98312 | tf_op jit(solution)/shard_map/ppermute | solution.py:23
  244.1 5.4 %collective-permute-start.23 = (f32[8,1,1024]{2,1,0:T(1,128)S(1)}, f32[8,1,1024]{2,1,0:T(1,128)S(1)}, u32[]{:S(2)}, u32[]{:S(2)}) collective-permute-start(f32[8,1,1024]{2,1,0:T(1,128)S(1)} %get-tuple-element.284), channel_id=1, source_target_pairs={{1,0},{2,1},{3,2},{4,3},{5,4},{6,5},{7,6},{9,8},{10,9},{11,10},{12... | collective-permute-start | bytes 98312 | tf_op jit(solution)/shard_map/ppermute | solution.py:23
  270.5 5.3 %collective-permute-start.25 = (f32[2,1,1024]{2,1,0:T(1,128)S(1)}, f32[2,1,1024]{2,1,0:T(1,128)S(1)}, u32[]{:S(2)}, u32[]{:S(2)}) collective-permute-start(f32[2,1,1024]{2,1,0:T(1,128)S(1)} %get-tuple-element.311), channel_id=1, source_target_pairs={{1,0},{2,1},{3,2},{4,3},{5,4},{6,5},{7,6},{9,8},{10,9},{11,10},{12... | collective-permute-start | bytes 24584 | tf_op jit(solution)/shard_map/ppermute | solution.py:23
  278.1 5.6 %collective-permute-start.27 = (f32[8,1,1024]{2,1,0:T(1,128)S(1)}, f32[8,1,1024]{2,1,0:T(1,128)S(1)}, u32[]{:S(2)}, u32[]{:S(2)}) collective-permute-start(f32[8,1,1024]{2,1,0:T(1,128)S(1)} %get-tuple-element.282), channel_id=1, source_target_pairs={{1,0},{2,1},{3,2},{4,3},{5,4},{6,5},{7,6},{9,8},{10,9},{11,10},{12... | collective-permute-start | bytes 98312 | tf_op jit(solution)/shard_map/ppermute | solution.py:23
  279.4 5.3 %collective-permute-start.28 = (f32[8,1,1024]{2,1,0:T(1,128)S(1)}, f32[8,1,1024]{2,1,0:T(1,128)S(1)}, u32[]{:S(2)}, u32[]{:S(2)}) collective-permute-start(f32[8,1,1024]{2,1,0:T(1,128)S(1)} %get-tuple-element.283), channel_id=1, source_target_pairs={{0,1},{1,2},{2,3},{3,4},{4,5},{5,6},{6,7},{8,9},{9,10},{10,11},{11... | collective-permute-start | bytes 98312 | tf_op jit(solution)/shard_map/ppermute | solution.py:20
  307.0 5.9 %collective-permute-start.29 = (f32[8,1,1024]{2,1,0:T(1,128)}, f32[8,1,1024]{2,1,0:T(1,128)}, u32[]{:S(2)}, u32[]{:S(2)}) collective-permute-start(f32[8,1,1024]{2,1,0:T(1,128)} %get-tuple-element.280), channel_id=1, source_target_pairs={{1,0},{2,1},{3,2},{4,3},{5,4},{6,5},{7,6},{9,8},{10,9},{11,10},{12... | collective-permute-start | bytes 98312 | tf_op jit(solution)/shard_map/ppermute | solution.py:23
  308.3 5.3 %collective-permute-start.30 = (f32[8,1,1024]{2,1,0:T(1,128)}, f32[8,1,1024]{2,1,0:T(1,128)}, u32[]{:S(2)}, u32[]{:S(2)}) collective-permute-start(f32[8,1,1024]{2,1,0:T(1,128)} %get-tuple-element.281), channel_id=1, source_target_pairs={{0,1},{1,2},{2,3},{3,4},{4,5},{5,6},{6,7},{8,9},{9,10},{10,11},{11... | collective-permute-start | bytes 98312 | tf_op jit(solution)/shard_map/ppermute | solution.py:20
  336.2 5.4 %collective-permute-start.31 = (f32[8,1,1024]{2,1,0:T(1,128)S(1)}, f32[8,1,1024]{2,1,0:T(1,128)S(1)}, u32[]{:S(2)}, u32[]{:S(2)}) collective-permute-start(f32[8,1,1024]{2,1,0:T(1,128)S(1)} %get-tuple-element.278), channel_id=1, source_target_pairs={{1,0},{2,1},{3,2},{4,3},{5,4},{6,5},{7,6},{9,8},{10,9},{11,10},{12... | collective-permute-start | bytes 98312 | tf_op jit(solution)/shard_map/ppermute | solution.py:23
  363.1 70.0 %collective-permute-start = (f32[2,16,1024]{2,1,0:T(8,128)S(1)}, f32[2,16,1024]{2,1,0:T(8,128)S(1)}, u32[]{:S(2)}, u32[]{:S(2)}) collective-permute-start(f32[2,16,1024]{2,1,0:T(8,128)S(1)} %get-tuple-element.634), channel_id=1, source_target_pairs={{0,8},{8,16},{16,24},{1,9},{9,17},{17,25},{2,10},{10,18},{18,26},{... | collective-permute-start | bytes 393224 | tf_op jit(solution)/shard_map/while/body/eval_jaxpr/ppermute | solution.py:31
  433.2 6.3 %collective-permute-start = (f32[2,16,1024]{2,1,0:T(8,128)S(1)}, f32[2,16,1024]{2,1,0:T(8,128)S(1)}, u32[]{:S(2)}, u32[]{:S(2)}) collective-permute-start(f32[2,16,1024]{2,1,0:T(8,128)S(1)} %get-tuple-element.634), channel_id=1, source_target_pairs={{0,8},{8,16},{16,24},{1,9},{9,17},{17,25},{2,10},{10,18},{18,26},{... | collective-permute-start | bytes 393224 | tf_op jit(solution)/shard_map/while/body/eval_jaxpr/ppermute | solution.py:31
  439.6 6.3 %collective-permute-start = (f32[2,16,1024]{2,1,0:T(8,128)S(1)}, f32[2,16,1024]{2,1,0:T(8,128)S(1)}, u32[]{:S(2)}, u32[]{:S(2)}) collective-permute-start(f32[2,16,1024]{2,1,0:T(8,128)S(1)} %get-tuple-element.634), channel_id=1, source_target_pairs={{0,8},{8,16},{16,24},{1,9},{9,17},{17,25},{2,10},{10,18},{18,26},{... | collective-permute-start | bytes 393224 | tf_op jit(solution)/shard_map/while/body/eval_jaxpr/ppermute | solution.py:31
  (37 other events, 112.3 us)
where the time goes:
time: 452 us; the launch traced here: 447 us
  blocking collectives  199 us (44%)
  waiting for transfers between devices  94.2 us (21%)
  starting transfers between devices  88.2 us (20%)
  other arithmetic  36.4 us (8%)
  between operations  16.8 us (4%)
  local copies, waits for them, and re-layouts  11.9 us (3%)
    psum x12, blocking collectives, global_products(): lax.psum((jnp.sum(residual * image), jnp.sum(image * image)), 'tile')  199 us
    ppermute x3, waiting for transfers between devices, shifted(): return lax.ppermute(block, axis, route)  78.7 us
    ppermute x16, starting transfers between devices, padded_2(): lax.ppermute(lax.slice_in_dim(block, block.shape[dim] - width, None, axis...  63.7 us
    ppermute x16, starting transfers between devices, padded_2(): lax.ppermute(lax.slice_in_dim(block, 0, width, axis=dim), axis, backward)  20.7 us
    reduce_sum x12, other arithmetic, global_products(): jnp.sum(image * image)  20.3 us
    ppermute x16, waiting for transfers between devices, padded_2(): lax.ppermute(lax.slice_in_dim(block, block.shape[dim] - width, None, axis...  12.4 us
    unnamed x136, local copies, waits for them, and re-layouts  9.32 us
  transfers between devices with their start and end apart: 35, of which 18 were waited for; matrix products, arithmetic and copies ran while one was open for 0% of the time, Pallas kernels for 0%

commit v1 on v0

v1 whole, which is shorter than its diff:
```python
import functools
import math

import jax
import jax.numpy as jnp
from jax import lax
from jax.experimental import pallas as pl
from jax.experimental.pallas import tpu as pltpu
from jax.sharding import PartitionSpec as P

LEVELS = 8
STAGES = 4
TIME_STEP = 0.8
SHIP_SPEED = 0.5
EPSILON = 1e-06
MESH = pl.DeviceIdType.MESH
SUB = 8
LANE = 128
REACH = 4
PACK = 8
NSUM = 10

THETA = [(m + 0.5) * math.pi / LEVELS for m in range(LEVELS)]
LAM = [2.0 * math.cos(t) - 2.0 for t in THETA]
WEIGHT = [(-1.0) ** m / math.tan(t / 2) / LEVELS for m, t in enumerate(THETA)]
TOPROW = [
    (math.cos((LEVELS - 2) * t) - 4.0 * math.cos((LEVELS - 1) * t)) * w
    for t, w in zip(THETA, WEIGHT)
]


def masks(shape):
    lane = lax.broadcasted_iota(jnp.int32, shape, len(shape) - 1)
    sub = lax.broadcasted_iota(jnp.int32, shape, len(shape) - 2)
    first = lane == 0
    last = lane == LANE - 1
    return first, first & (sub == 0), last, last & (sub == SUB - 1)


def before(v, mask):
    first, start, _, _ = mask
    r = pltpu.roll(v, 1, axis=2)
    return jnp.where(start, 0.0, jnp.where(first, pltpu.roll(r, 1, axis=1), r))


def after(v, mask):
    _, _, last, end = mask
    r = pltpu.roll(v, LANE - 1, axis=2)
    return jnp.where(end, 0.0, jnp.where(last, pltpu.roll(r, SUB - 1, axis=1), r))


def neighbours(v):
    mid = v[1:-1]
    mask = masks(mid.shape)
    return (v[2:] + v[:-2]) + (before(mid, mask) + after(mid, mask))


def step_sizes(g):
    g00, g01, g02, g03, g11, g12, g13, g22, g23, g33 = g
    gram = [[g00, g01, g02, g03], [g01, g11, g12, g13], [g02, g12, g22, g23], [g03, g13, g23, g33]]

    def quad(c, left, right):
        total = None
        for i, ci in enumerate(c):
            for j, cj in enumerate(c):
                if left == right and j < i:
                    continue
                term = ci * cj * gram[i + left][j + right]
                if left == right and j > i:
                    term = 2.0 * term
                total = term if total is None else total + term
        return total

    coef = [jnp.ones_like(g00)]
    beta = [0.0, 0.0, 0.0]
    for sweep in range(3):
        rr = quad(coef, 0, 0)
        re = quad(coef, 0, 1)
        ee = quad(coef, 1, 1)
        inv = 1.0 / (jnp.maximum(rr + 2.0 * re + ee, 0.0) + EPSILON)
        s = (rr + re) * inv
        t = (re + ee + EPSILON) * inv
        for j, c in enumerate(coef):
            beta[j] = beta[j] + s * c
        nxt = [t * c for c in coef] + [jnp.zeros_like(s)]
        for j, c in enumerate(coef):
            nxt[j + 1] = nxt[j + 1] - s * c
        coef = nxt
    return beta


def kernel(
    tiles, slices, rows, state_ref, depth_ref, press_ref, out_ref,
    st, dep, prs, dm, coarse, first, total, planes, pack, halo, part, slots, chain, chain_in,
    halo_s, halo_r, sum_s, sum_r, chain_s, chain_r,
):
    me = lax.axis_index("tile")
    cut = lax.axis_index("cuts")
    has_lo = me > 0
    has_hi = me < tiles - 1
    has_prev = cut > 0
    has_next = cut < slices - 1
    chunks = [(a, min(4, rows - a)) for a in range(0, rows, 4)]

    halo[...] = jnp.zeros_like(halo)

    barrier = pltpu.get_barrier_semaphore()
    for d in range(1, tiles):
        pl.semaphore_signal(
            barrier, inc=1, device_id={"tile": lax.rem(me + d, tiles)}, device_id_type=MESH
        )

    @pl.when(has_prev)
    def _():
        pl.semaphore_signal(barrier, inc=1, device_id={"cuts": cut - 1}, device_id_type=MESH)

    @pl.when(has_next)
    def _():
        pl.semaphore_signal(barrier, inc=1, device_id={"cuts": cut + 1}, device_id_type=MESH)

    for j in range(SUB):
        cols = slice(j * LANE, (j + 1) * LANE)
        for c in range(2):
            st[c, :, j, :] = state_ref[0, c, :, cols]
        dep[3 : 3 + rows, j, :] = depth_ref[:, cols]
        prs[:, j, :] = press_ref[:, cols]

    first[...] = st[...]

    def halo_copy(s, side, count):
        return pltpu.make_async_remote_copy(
            src_ref=pack.at[s, side, pl.ds(0, count)],
            dst_ref=halo.at[s, 1 - side, pl.ds(0, count)],
            send_sem=halo_s.at[s, side],
            recv_sem=halo_r.at[s, 1 - side],
            device_id={"tile": me - 1 if side == 0 else me + 1},
            device_id_type=MESH,
        )

    def halo_both(s, count, act):
        @pl.when(has_lo)
        def _():
            act(halo_copy, s, 0, count)

        @pl.when(has_hi)
        def _():
            act(halo_copy, s, 1, count)

    start = lambda copy, s, side, count: copy(s, side, count).start()
    arrive = lambda copy, s, side, count: copy(s, 1 - side, count).wait_recv()
    leave = lambda copy, s, side, count: copy(s, side, count).wait_send()

    def fill(s):
        pack[s, 0, 0:4] = st[1, 0:4]
        pack[s, 0, 4:5] = st[0, 0:1]
        pack[s, 1, 0:4] = st[1, rows - 4 : rows]
        pack[s, 1, 4:5] = st[0, rows - 1 : rows]

    fill(0)
    pack[0, 0, 5:8] = dep[3:6]
    pack[0, 1, 5:8] = dep[rows : rows + 3]
    pl.semaphore_wait(
        barrier, tiles - 1 + has_prev.astype(jnp.int32) + has_next.astype(jnp.int32)
    )
    halo_both(0, 8, start)

    own = dep[3 : 3 + rows]
    stiff = jnp.tanh(own)
    z = TIME_STEP * TIME_STEP * stiff
    cosine = 1.0 + z * (-1 / 2 + z * (1 / 24 + z * (-1 / 720 + z * (1 / 40320 - z / 3628800))))
    sine = TIME_STEP * (
        1.0 + z * (-1 / 6 + z * (1 / 120 + z * (-1 / 5040 + z * (1 / 362880 - z / 39916800))))
    )
    coarse[0] = cosine
    coarse[1] = stiff * sine
    coarse[2] = -sine

    halo_both(0, 8, arrive)
    dep[0:3] = halo[0, 0, 5:8]
    dep[rows + 3 : rows + 6] = halo[0, 1, 5:8]
    wide = dep[...]
    row = lax.broadcasted_iota(jnp.int32, wide.shape, 0)
    inside = (has_lo | (row >= 3)) & (has_hi | (row < rows + 3))
    safe = jnp.where(inside, wide, 1.0)
    vert = LEVELS / safe
    vert = vert * vert
    for m in range(LEVELS):
        dm[m] = jnp.where(inside, 1.0 / (vert * LAM[m] - 4.0), 0.0)
    dep[3 : 3 + rows] = (0.5 * LEVELS) / safe[3 : 3 + rows]

    def sum_copy(s, d):
        return pltpu.make_async_remote_copy(
            src_ref=part.at[s],
            dst_ref=slots.at[s, d],
            send_sem=sum_s.at[s, d],
            recv_sem=sum_r.at[s, d],
            device_id={"tile": lax.rem(me + d, tiles)},
            device_id_type=MESH,
        )

    def stage(s, carry):
        lo = halo[s, 0, 0:5]
        hi = halo[s, 1, 0:5]
        top = jnp.concatenate([lo[0:4], st[1], hi[0:4]], axis=0)
        r0 = 4.0 * top[1:-1] - neighbours(top)
        u0 = r0[3:-3]
        gram = [None] * 9
        for m in range(LEVELS):
            c0 = dm[m] * r0
            u1 = neighbours(c0)
            c1 = dm[m, 1:-1] * u1
            u2 = neighbours(c1)
            c2 = dm[m, 2:-2] * u2
            u3 = neighbours(c2)
            us = [u0, u1[2:-2], u2[1:-1], u3]
            cs = [c0[3:-3], c1[2:-2], c2[1:-1]]
            k = 0
            for i in range(4):
                for j in range(max(i, 1), 4):
                    p = (4.0 * WEIGHT[m] ** 2) * jnp.sum(us[i] * us[j], axis=0)
                    gram[k] = p if gram[k] is None else gram[k] + p
                    k += 1
            for i in range(3):
                a = WEIGHT[m] * us[i + 1]
                b = TOPROW[m] * cs[i]
                if m == 0:
                    planes[i] = a
                    planes[3 + i] = b
                else:
                    planes[i] += a
                    planes[3 + i] += b
        bottom = [u0, planes[0], planes[1], planes[2]]
        k = 0
        for i in range(4):
            for j in range(max(i, 1), 4):
                gram[k] = gram[k] + 0.5 * jnp.sum(bottom[i] * bottom[j], axis=0)
                k += 1
        gram = [LEVELS * jnp.sum(u0 * u0, axis=0)] + gram
        for k in range(NSUM):
            part[s, k : k + 1] = jnp.sum(gram[k], axis=0, keepdims=True)
        for k in range(NSUM, 16):
            part[s, k : k + 1] = jnp.zeros((1, LANE), jnp.float32)
        for d in range(1, tiles):
            sum_copy(s, d).start()

        elev = st[0]
        phi = st[1]
        tall = jnp.concatenate([lo[4:5], elev, hi[4:5]], axis=0)
        mask = masks(elev.shape)
        he = 0.5 * (tall[2:] - tall[:-2])
        fe = 0.5 * (top[5:-3] - top[3:-5])
        hn = 0.5 * (after(elev, mask) - before(elev, mask))
        fn = 0.5 * (after(phi, mask) - before(phi, mask))
        slope = 1.0 + he * he + hn * hn
        rate_h = SHIP_SPEED * he - (he * fe + hn * fn)
        rate_f = SHIP_SPEED * fe - elev - 0.5 * (fe * fe + fn * fn) - prs[...]

        for d in range(1, tiles):
            sum_copy(s, d).wait_recv()
        whole = part[s]
        for d in range(1, tiles):
            whole = whole + slots[s, d]
        whole = jnp.sum(whole, axis=1, keepdims=True)
        beta = step_sizes([whole[k : k + 1] for k in range(NSUM)])
        beta = [jnp.broadcast_to(b, (SUB, LANE)) for b in beta]
        w = (beta[0] * planes[3] + beta[1] * planes[4] + beta[2] * planes[5]) * dep[3 : 3 + rows]
        ws = w * slope
        rate_h = rate_h + ws
        rate_f = rate_f + 0.5 * w * ws

        share = jnp.where((s == 0) | (s == STAGES - 1), 1.0, 2.0) * (TIME_STEP / 6.0)
        ahead = jnp.where(s == STAGES - 2, TIME_STEP, 0.5 * TIME_STEP)

        @pl.when(s == 0)
        def _():
            total[...] = first[...]

        total[0] += share * rate_h
        total[1] += share * rate_f
        st[0] = first[0] + ahead * rate_h
        st[1] = first[1] + ahead * rate_f

        @pl.when(s < STAGES - 1)
        def _():
            fill(s + 1)
            halo_both(s + 1, 5, start)
            halo_both(s + 1, 5, arrive)

        return carry

    lax.fori_loop(0, STAGES, stage, 0)

    def chain_copy(k):
        a, size = chunks[k]
        return pltpu.make_async_remote_copy(
            src_ref=chain.at[pl.ds(a, size)],
            dst_ref=chain_in.at[pl.ds(a, size)],
            send_sem=chain_s.at[k],
            recv_sem=chain_r.at[k],
            device_id={"cuts": cut + 1},
            device_id_type=MESH,
        )

    @pl.when(has_prev)
    def _():
        total[0] = total[0] - (coarse[0] * first[0] + coarse[1] * first[1])
        total[1] = total[1] - (coarse[2] * first[0] + coarse[0] * first[1])

    for k, (a, size) in enumerate(chunks):
        span = slice(a, a + size)

        @pl.when(has_prev)
        def _():
            chain_copy(k).wait_recv()
            e = chain_in[span, 0]
            p = chain_in[span, 1]
            chain[span, 0] = coarse[0, span] * e + coarse[1, span] * p + total[0, span]
            chain[span, 1] = coarse[2, span] * e + coarse[0, span] * p + total[1, span]

        @pl.when(jnp.logical_not(has_prev))
        def _():
            chain[span, 0] = total[0, span]
            chain[span, 1] = total[1, span]

        @pl.when(has_next)
        def _():
            chain_copy(k).start()

    for j in range(SUB):
        cols = slice(j * LANE, (j + 1) * LANE)
        for c in range(2):
            out_ref[0, c, :, cols] = chain[:, c, j, :]

    @pl.when(has_next)
    def _():
        for k in range(len(chunks)):
            chain_copy(k).wait_send()

    halo_both(0, 8, leave)
    for s in range(1, STAGES):
        halo_both(s, 5, leave)
    for s in range(STAGES):
        for d in range(1, tiles):
            sum_copy(s, d).wait_send()


def local(tiles, slices, state_in, sea_depth, pressure):
    rows = sea_depth.shape[0]
    plane = (rows, SUB, LANE)
    f32 = jnp.float32
    chunks = -(-rows // 4)
    return pl.pallas_call(
        functools.partial(kernel, tiles, slices, rows),
        out_shape=jax.ShapeDtypeStruct(state_in.shape, f32),
        in_specs=[pl.BlockSpec(memory_space=pltpu.VMEM)] * 3,
        out_specs=pl.BlockSpec(memory_space=pltpu.VMEM),
        scratch_shapes=[
            pltpu.VMEM((2,) + plane, f32),
            pltpu.VMEM((rows + 6, SUB, LANE), f32),
            pltpu.VMEM(plane, f32),
            pltpu.VMEM((LEVELS, rows + 6, SUB, LANE), f32),
            pltpu.VMEM((3,) + plane, f32),
            pltpu.VMEM((2,) + plane, f32),
            pltpu.VMEM((2,) + plane, f32),
            pltpu.VMEM((6,) + plane, f32),
            pltpu.VMEM((STAGES, 2, PACK, SUB, LANE), f32),
            pltpu.VMEM((STAGES, 2, PACK, SUB, LANE), f32),
            pltpu.VMEM((STAGES, 16, LANE), f32),
            pltpu.VMEM((STAGES, tiles, 16, LANE), f32),
            pltpu.VMEM((rows, 2, SUB, LANE), f32),
            pltpu.VMEM((rows, 2, SUB, LANE), f32),
            pltpu.SemaphoreType.DMA((STAGES, 2)),
            pltpu.SemaphoreType.DMA((STAGES, 2)),
            pltpu.SemaphoreType.DMA((STAGES, tiles)),
            pltpu.SemaphoreType.DMA((STAGES, tiles)),
            pltpu.SemaphoreType.DMA((chunks,)),
            pltpu.SemaphoreType.DMA((chunks,)),
        ],
        compiler_params=pltpu.CompilerParams(
            collective_id=0, has_side_effects=True, vmem_limit_bytes=48 * 1024 * 1024
        ),
        name="wake_step",
    )(state_in, sea_depth, pressure)


def solution(mesh):
    placed = (P("cuts", None, "tile", None), P("tile", None), P("tile", None))
    return jax.shard_map(
        functools.partial(local, mesh.shape["tile"], mesh.shape["cuts"]),
        mesh=mesh,
        in_specs=placed,
        out_specs=P("cuts", None, "tile", None),
        check_vma=False,
    )
```

time: 452 us -> 52.9 us (0.12); the launches traced: 447 us -> 52.6 us
  blocking collectives: 199 us -> 0 us
  waiting for transfers between devices: 94.2 us -> 0 us
  starting transfers between devices: 88.2 us -> 0 us
  Pallas kernels: 0 us -> 49.4 us
  other arithmetic: 36.4 us -> 0 us
  between operations: 16.8 us -> 0.01 us
  local copies, waits for them, and re-layouts: 11.9 us -> 3.24 us
    psum x12 -> x0, blocking collectives: 199 us -> none  [global_products(): lax.psum((jnp.sum(residual * image), jnp.sum(image * image)), 'tile')]
    ppermute x35 -> x0, waiting for transfers between devices: 94.2 us -> none  [the longest x3 78.7 us: shifted(): return lax.ppermute(block, axis, route)]
    ppermute x35 -> x0, starting transfers between devices: 88.2 us -> none  [the longest x16 63.7 us: padded_2(): lax.ppermute(lax.slice_in_dim(block, block.shape[dim] - width, None, axis...]
    pallas_call x0 -> x1, Pallas kernels: none -> 49.4 us  [local(): pl.pallas_call(functools.partial(kernel, tiles, slices, rows), out_shape=...]
    reduce_sum x12 -> x0, other arithmetic: 20.3 us -> none  [global_products(): jnp.sum(image * image)]
    sub x8 -> x0, other arithmetic: 6.93 us -> none  [solve_narrow(): residual = residual - step_size * image]
    unnamed x136 -> x7, local copies, waits for them, and re-layouts: 9.32 us -> 3.24 us
  transfers between devices with their start and end apart: 35 -> 0, of which waited for: 18 -> 0; matrix products, arithmetic and copies ran while one was open for 0% -> 0% of each run, Pallas kernels for 0% -> 0%
where the time goes in v1:
time: 52.9 us; the launch traced here: 52.6 us
  Pallas kernels  49.4 us (93%)
  local copies, waits for them, and re-layouts  3.24 us (6%)
    pallas_call x1, Pallas kernels, local(): pl.pallas_call(functools.partial(kernel, tiles, slices, rows), out_shape=...  49.4 us
    unnamed x7, local copies, waits for them, and re-layouts  3.24 us

profile of v1, /device:TPU:3, one launch (start us, length us, event | category | flops | bytes accessed | tf_op | source)
XLA Modules:
  0.0 52.6 jit_solution(10783086330046764587)
XLA Ops:
  0.0 0.0 copy-start
  0.0 0.9 %copy-done = f32[1,2,16,1024]{3,2,1,0:T(8,128)S(1)} copy-done((f32[1,2,16,1024]{3,2,1,0:T(8,128)S(1)}, f32[1,2,16,1024]{3,2,1,0:T(8,128)}, u32[]{:S(2)}) %copy-start) | copy-done | bytes 131096
  0.9 0.0 copy-start.1
  0.9 0.8 %copy-done.1 = f32[16,1024]{1,0:T(8,128)S(1)} copy-done((f32[16,1024]{1,0:T(8,128)S(1)}, f32[16,1024]{1,0:T(8,128)}, u32[]{:S(2)}) %copy-start.1) | copy-done | bytes 65560
  1.7 0.0 copy-start.2
  1.7 0.8 %copy-done.2 = f32[16,1024]{1,0:T(8,128)S(1)} copy-done((f32[16,1024]{1,0:T(8,128)S(1)}, f32[16,1024]{1,0:T(8,128)}, u32[]{:S(2)}) %copy-start.2) | copy-done | bytes 65560
  2.6 49.4 %wake_step.1 = f32[1,2,16,1024]{3,2,1,0:T(8,128)S(1)} custom-call(f32[1,2,16,1024]{3,2,1,0:T(8,128)S(1)} %copy-done, f32[16,1024]{1,0:T(8,128)S(1)} %copy-done.1, f32[16,1024]{1,0:T(8,128)S(1)} %copy-done.2), custom_call_target="tpu_custom_call" | custom-call | tf_op jit(solution)/shard_map/wake_step/pallas_call | solution.py:352
  52.0 0.7 %copy.5 = f32[1,2,16,1024]{3,2,1,0:T(8,128)} copy(f32[1,2,16,1024]{3,2,1,0:T(8,128)S(1)} %wake_step.1) | data formatting | bytes 262144
Async XLA Ops:
  0.0 0.9 %copy-start = (f32[1,2,16,1024]{3,2,1,0:T(8,128)S(1)}, f32[1,2,16,1024]{3,2,1,0:T(8,128)}, u32[]{:S(2)}) copy-start(f32[1,2,16,1024]{3,2,1,0:T(8,128)} %state_ref.1) | copy-start | bytes 393220
  0.9 0.8 %copy-start.1 = (f32[16,1024]{1,0:T(8,128)S(1)}, f32[16,1024]{1,0:T(8,128)}, u32[]{:S(2)}) copy-start(f32[16,1024]{1,0:T(8,128)} %depth_ref.1) | copy-start | bytes 196612
  1.7 0.8 %copy-start.2 = (f32[16,1024]{1,0:T(8,128)S(1)}, f32[16,1024]{1,0:T(8,128)}, u32[]{:S(2)}) copy-start(f32[16,1024]{1,0:T(8,128)} %press_ref.1) | copy-start | bytes 196612

commit v2 on v1

--- a/solution.py
+++ b/solution.py
@@ -16,9 +16,10 @@
 MESH = pl.DeviceIdType.MESH
 SUB = 8
 LANE = 128
-REACH = 4
-PACK = 8
 NSUM = 10
+FOLD = 5
+WIDE = 13
+EXTRA = [10, 7, 4, 0]
 
 THETA = [(m + 0.5) * math.pi / LEVELS for m in range(LEVELS)]
 LAM = [2.0 * math.cos(t) - 2.0 for t in THETA]
@@ -91,8 +92,8 @@
 
 def kernel(
     tiles, slices, rows, state_ref, depth_ref, press_ref, out_ref,
-    st, dep, prs, dm, coarse, first, total, planes, pack, halo, part, slots, chain, chain_in,
-    halo_s, halo_r, sum_s, sum_r, chain_s, chain_r,
+    raw, raw_d, raw_p, x, dm, wfac, coarse, first, total, planes, edge, part, slots, chain, chain_in,
+    load_s, halo_s, halo_r, sum_s, sum_r, chain_s, chain_r,
 ):
     me = lax.axis_index("tile")
     cut = lax.axis_index("cuts")
@@ -101,8 +102,18 @@
     has_prev = cut > 0
     has_next = cut < slices - 1
     chunks = [(a, min(4, rows - a)) for a in range(0, rows, 4)]
-
-    halo[...] = jnp.zeros_like(halo)
+    end = WIDE + rows
+
+    loads = [
+        pltpu.make_async_copy(state_ref.at[0], raw, load_s.at[0]),
+        pltpu.make_async_copy(depth_ref, raw_d, load_s.at[1]),
+        pltpu.make_async_copy(press_ref, raw_p, load_s.at[2]),
+    ]
+    for load in loads:
+        load.start()
+
+    x[:, 0:WIDE] = jnp.zeros((4, WIDE, SUB, LANE), jnp.float32)
+    x[:, end : end + WIDE] = jnp.zeros((4, WIDE, SUB, LANE), jnp.float32)
 
     barrier = pltpu.get_barrier_semaphore()
     for d in range(1, tiles):
@@ -118,53 +129,64 @@
     def _():
         pl.semaphore_signal(barrier, inc=1, device_id={"cuts": cut + 1}, device_id_type=MESH)
 
+    for load in loads:
+        load.wait()
     for j in range(SUB):
         cols = slice(j * LANE, (j + 1) * LANE)
-        for c in range(2):
-            st[c, :, j, :] = state_ref[0, c, :, cols]
-        dep[3 : 3 + rows, j, :] = depth_ref[:, cols]
-        prs[:, j, :] = press_ref[:, cols]
-
-    first[...] = st[...]
-
-    def halo_copy(s, side, count):
+        x[0, WIDE:end, j, :] = raw[1, :, cols]
+        x[1, WIDE:end, j, :] = raw_d[:, cols]
+        x[2, WIDE:end, j, :] = raw[0, :, cols]
+        x[3, WIDE:end, j, :] = raw_p[:, cols]
+
+    parts = [(0, 2, 0, 4), (0, 2, 4, WIDE - 4), (2, 2, 0, WIDE - 2)]
+
+    def halo_copy(k, side):
+        p, np_, a, size = parts[k]
+        if side == 0:
+            src, dst = WIDE + a, end + a
+        else:
+            src, dst = end - a - size, WIDE - a - size
         return pltpu.make_async_remote_copy(
-            src_ref=pack.at[s, side, pl.ds(0, count)],
-            dst_ref=halo.at[s, 1 - side, pl.ds(0, count)],
-            send_sem=halo_s.at[s, side],
-            recv_sem=halo_r.at[s, 1 - side],
+            src_ref=x.at[pl.ds(p, np_), pl.ds(src, size)],
+            dst_ref=x.at[pl.ds(p, np_), pl.ds(dst, size)],
+            send_sem=halo_s.at[k, side],
+            recv_sem=halo_r.at[k, side],
             device_id={"tile": me - 1 if side == 0 else me + 1},
             device_id_type=MESH,
         )
 
-    def halo_both(s, count, act):
+    def halo_both(k, act):
         @pl.when(has_lo)
         def _():
-            act(halo_copy, s, 0, count)
+            act(k, 0)
 
         @pl.when(has_hi)
         def _():
-            act(halo_copy, s, 1, count)
-
-    start = lambda copy, s, side, count: copy(s, side, count).start()
-    arrive = lambda copy, s, side, count: copy(s, 1 - side, count).wait_recv()
-    leave = lambda copy, s, side, count: copy(s, side, count).wait_send()
-
-    def fill(s):
-        pack[s, 0, 0:4] = st[1, 0:4]
-        pack[s, 0, 4:5] = st[0, 0:1]
-        pack[s, 1, 0:4] = st[1, rows - 4 : rows]
-        pack[s, 1, 4:5] = st[0, rows - 1 : rows]
-
-    fill(0)
-    pack[0, 0, 5:8] = dep[3:6]
-    pack[0, 1, 5:8] = dep[rows : rows + 3]
+            act(k, 1)
+
+    start = lambda k, side: halo_copy(k, side).start()
+    arrive = lambda k, side: halo_copy(k, 1 - side).wait_recv()
+    leave = lambda k, side: halo_copy(k, side).wait_send()
+
+    def columns(a, b, inside):
+        safe = x[1, a:b]
+        if inside is not None:
+            safe = jnp.where(inside, safe, 1.0)
+        vert = LEVELS / safe
+        vert = vert * vert
+        for m in range(LEVELS):
+            inverse = 1.0 / (vert * LAM[m] - 4.0)
+            dm[m, a:b] = inverse if inside is None else jnp.where(inside, inverse, 0.0)
+        wfac[a:b] = (0.5 * LEVELS) / safe
+
     pl.semaphore_wait(
         barrier, tiles - 1 + has_prev.astype(jnp.int32) + has_next.astype(jnp.int32)
     )
-    halo_both(0, 8, start)
-
-    own = dep[3 : 3 + rows]
+    for k in range(3):
+        halo_both(k, start)
+
+    columns(WIDE, end, None)
+    own = x[1, WIDE:end]
     stiff = jnp.tanh(own)
     z = TIME_STEP * TIME_STEP * stiff
     cosine = 1.0 + z * (-1 / 2 + z * (1 / 24 + z * (-1 / 720 + z * (1 / 40320 - z / 3628800))))
@@ -175,18 +197,9 @@
     coarse[1] = stiff * sine
     coarse[2] = -sine
 
-    halo_both(0, 8, arrive)
-    dep[0:3] = halo[0, 0, 5:8]
-    dep[rows + 3 : rows + 6] = halo[0, 1, 5:8]
-    wide = dep[...]
-    row = lax.broadcasted_iota(jnp.int32, wide.shape, 0)
-    inside = (has_lo | (row >= 3)) & (has_hi | (row < rows + 3))
-    safe = jnp.where(inside, wide, 1.0)
-    vert = LEVELS / safe
-    vert = vert * vert
-    for m in range(LEVELS):
-        dm[m] = jnp.where(inside, 1.0 / (vert * LAM[m] - 4.0), 0.0)
-    dep[3 : 3 + rows] = (0.5 * LEVELS) / safe[3 : 3 + rows]
+    halo_both(0, arrive)
+    columns(WIDE - 3, WIDE, has_lo)
+    columns(end, end + 3, has_hi)
 
     def sum_copy(s, d):
         return pltpu.make_async_remote_copy(
@@ -198,19 +211,19 @@
             device_id_type=MESH,
         )
 
-    def stage(s, carry):
-        lo = halo[s, 0, 0:5]
-        hi = halo[s, 1, 0:5]
-        top = jnp.concatenate([lo[0:4], st[1], hi[0:4]], axis=0)
+    half = lax.broadcasted_iota(jnp.int32, (1, LANE), 1) < LANE // 2
+
+    def inner_products(s):
+        top = x[0, WIDE - 4 : end + 4]
         r0 = 4.0 * top[1:-1] - neighbours(top)
         u0 = r0[3:-3]
         gram = [None] * 9
         for m in range(LEVELS):
-            c0 = dm[m] * r0
+            c0 = dm[m, WIDE - 3 : end + 3] * r0
             u1 = neighbours(c0)
-            c1 = dm[m, 1:-1] * u1
+            c1 = dm[m, WIDE - 2 : end + 2] * u1
             u2 = neighbours(c1)
-            c2 = dm[m, 2:-2] * u2
+            c2 = dm[m, WIDE - 1 : end + 1] * u2
             u3 = neighbours(c2)
             us = [u0, u1[2:-2], u2[1:-1], u3]
             cs = [c0[3:-3], c1[2:-2], c2[1:-1]]
@@ -236,59 +249,101 @@
                 gram[k] = gram[k] + 0.5 * jnp.sum(bottom[i] * bottom[j], axis=0)
                 k += 1
         gram = [LEVELS * jnp.sum(u0 * u0, axis=0)] + gram
-        for k in range(NSUM):
-            part[s, k : k + 1] = jnp.sum(gram[k], axis=0, keepdims=True)
-        for k in range(NSUM, 16):
-            part[s, k : k + 1] = jnp.zeros((1, LANE), jnp.float32)
-        for d in range(1, tiles):
-            sum_copy(s, d).start()
-
-        elev = st[0]
-        phi = st[1]
-        tall = jnp.concatenate([lo[4:5], elev, hi[4:5]], axis=0)
+        gram = [jnp.sum(g, axis=0, keepdims=True) for g in gram]
+        for k in range(FOLD):
+            a, b = gram[k], gram[k + FOLD]
+            part[s, k : k + 1] = jnp.where(half, a, b) + pltpu.roll(
+                jnp.where(half, b, a), LANE // 2, axis=1
+            )
+
+    def beyond(side, a, b):
+        top = x[0, a - 3 : b + 3]
+        r0 = 4.0 * top[1:-1] - neighbours(top)
+        size = b - a
+        for m in range(LEVELS):
+            c0 = dm[m, a - 2 : b + 2] * r0
+            c1 = dm[m, a - 1 : b + 1] * neighbours(c0)
+            c2 = dm[m, a:b] * neighbours(c1)
+            for i, c in enumerate([c0[2:-2], c1[1:-1], c2]):
+                v = TOPROW[m] * c
+                if m == 0:
+                    edge[side, i, 0:size] = v
+                else:
+                    edge[side, i, 0:size] += v
+
+    def explicit(a, b):
+        elev = x[2, a:b]
+        phi = x[0, a:b]
         mask = masks(elev.shape)
-        he = 0.5 * (tall[2:] - tall[:-2])
-        fe = 0.5 * (top[5:-3] - top[3:-5])
+        he = 0.5 * (x[2, a + 1 : b + 1] - x[2, a - 1 : b - 1])
+        fe = 0.5 * (x[0, a + 1 : b + 1] - x[0, a - 1 : b - 1])
         hn = 0.5 * (after(elev, mask) - before(elev, mask))
         fn = 0.5 * (after(phi, mask) - before(phi, mask))
         slope = 1.0 + he * he + hn * hn
         rate_h = SHIP_SPEED * he - (he * fe + hn * fn)
-        rate_f = SHIP_SPEED * fe - elev - 0.5 * (fe * fe + fn * fn) - prs[...]
+        rate_f = SHIP_SPEED * fe - elev - 0.5 * (fe * fe + fn * fn) - x[3, a:b]
+        return slope, rate_h, rate_f
+
+    for s in range(STAGES):
+        extra = EXTRA[s]
+        inner_products(s)
+        for d in range(1, tiles):
+            sum_copy(s, d).start()
+
+        if s == 0:
+            halo_both(1, arrive)
+            halo_both(2, arrive)
+            columns(1, WIDE - 3, has_lo)
+            columns(end + 3, end + WIDE - 1, has_hi)
+            first[0] = x[2]
+            first[1] = x[0]
+        regions = [(WIDE, end, None)]
+        if extra:
+            beyond(0, WIDE - extra, WIDE)
+            beyond(1, end, end + extra)
+            regions += [(WIDE - extra, WIDE, 0), (end, end + extra, 1)]
+        known = [explicit(a, b) for a, b, _ in regions]
+        if s == 0:
+            for k in range(3):
+                halo_both(k, leave)
 
         for d in range(1, tiles):
             sum_copy(s, d).wait_recv()
         whole = part[s]
         for d in range(1, tiles):
             whole = whole + slots[s, d]
-        whole = jnp.sum(whole, axis=1, keepdims=True)
-        beta = step_sizes([whole[k : k + 1] for k in range(NSUM)])
-        beta = [jnp.broadcast_to(b, (SUB, LANE)) for b in beta]
-        w = (beta[0] * planes[3] + beta[1] * planes[4] + beta[2] * planes[5]) * dep[3 : 3 + rows]
-        ws = w * slope
-        rate_h = rate_h + ws
-        rate_f = rate_f + 0.5 * w * ws
-
-        share = jnp.where((s == 0) | (s == STAGES - 1), 1.0, 2.0) * (TIME_STEP / 6.0)
-        ahead = jnp.where(s == STAGES - 2, TIME_STEP, 0.5 * TIME_STEP)
-
-        @pl.when(s == 0)
-        def _():
-            total[...] = first[...]
-
-        total[0] += share * rate_h
-        total[1] += share * rate_f
-        st[0] = first[0] + ahead * rate_h
-        st[1] = first[1] + ahead * rate_f
-
-        @pl.when(s < STAGES - 1)
-        def _():
-            fill(s + 1)
-            halo_both(s + 1, 5, start)
-            halo_both(s + 1, 5, arrive)
-
-        return carry
-
-    lax.fori_loop(0, STAGES, stage, 0)
+        low = jnp.sum(jnp.where(half, whole, 0.0), axis=1, keepdims=True)
+        high = jnp.sum(jnp.where(half, 0.0, whole), axis=1, keepdims=True)
+        sums = [low[k : k + 1] for k in range(FOLD)] + [high[k : k + 1] for k in range(FOLD)]
+        beta = [jnp.broadcast_to(b, (SUB, LANE)) for b in step_sizes(sums)]
+
+        share = (1.0 if s in (0, STAGES - 1) else 2.0) * (TIME_STEP / 6.0)
+        ahead = TIME_STEP if s == STAGES - 2 else 0.5 * TIME_STEP
+        for (a, b, side), (slope, rate_h, rate_f) in zip(regions, known):
+            if side is None:
+                y = [planes[3 + i] for i in range(3)]
+            else:
+                y = [edge[side, i, 0 : b - a] for i in range(3)]
+            w = (beta[0] * y[0] + beta[1] * y[1] + beta[2] * y[2]) * wfac[a:b]
+            ws = w * slope
+            rate_h = rate_h + ws
+            rate_f = rate_f + 0.5 * w * ws
+            if side is None:
+                if s == 0:
+                    total[0] = first[0, a:b] + share * rate_h
+                    total[1] = first[1, a:b] + share * rate_f
+                else:
+                    total[0] += share * rate_h
+                    total[1] += share * rate_f
+            if s < STAGES - 1:
+                new_h = first[0, a:b] + ahead * rate_h
+                new_f = first[1, a:b] + ahead * rate_f
+                if side is not None:
+                    there = has_hi if side else has_lo
+                    new_h = jnp.where(there, new_h, 0.0)
+                    new_f = jnp.where(there, new_f, 0.0)
+                x[2, a:b] = new_h
+                x[0, a:b] = new_f
 
     def chain_copy(k):
         a, size = chunks[k]
@@ -303,8 +358,10 @@
 
     @pl.when(has_prev)
     def _():
-        total[0] = total[0] - (coarse[0] * first[0] + coarse[1] * first[1])
-        total[1] = total[1] - (coarse[2] * first[0] + coarse[0] * first[1])
+        e = first[0, WIDE:end]
+        p = first[1, WIDE:end]
+        total[0] = total[0] - (coarse[0] * e + coarse[1] * p)
+        total[1] = total[1] - (coarse[2] * e + coarse[0] * p)
 
     for k, (a, size) in enumerate(chunks):
         span = slice(a, a + size)
@@ -336,9 +393,6 @@
         for k in range(len(chunks)):
             chain_copy(k).wait_send()
 
-    halo_both(0, 8, leave)
-    for s in range(1, STAGES):
-        halo_both(s, 5, leave)
     for s in range(STAGES):
         for d in range(1, tiles):
             sum_copy(s, d).wait_send()
@@ -347,30 +401,33 @@
 def local(tiles, slices, state_in, sea_depth, pressure):
     rows = sea_depth.shape[0]
     plane = (rows, SUB, LANE)
+    wide = rows + 2 * WIDE
     f32 = jnp.float32
     chunks = -(-rows // 4)
     return pl.pallas_call(
         functools.partial(kernel, tiles, slices, rows),
         out_shape=jax.ShapeDtypeStruct(state_in.shape, f32),
-        in_specs=[pl.BlockSpec(memory_space=pltpu.VMEM)] * 3,
+        in_specs=[pl.BlockSpec(memory_space=pltpu.HBM)] * 3,
         out_specs=pl.BlockSpec(memory_space=pltpu.VMEM),
         scratch_shapes=[
-            pltpu.VMEM((2,) + plane, f32),
-            pltpu.VMEM((rows + 6, SUB, LANE), f32),
-            pltpu.VMEM(plane, f32),
-            pltpu.VMEM((LEVELS, rows + 6, SUB, LANE), f32),
+            pltpu.VMEM(state_in.shape[1:], f32),
+            pltpu.VMEM(sea_depth.shape, f32),
+            pltpu.VMEM(pressure.shape, f32),
+            pltpu.VMEM((4, wide, SUB, LANE), f32),
+            pltpu.VMEM((LEVELS, wide, SUB, LANE), f32),
+            pltpu.VMEM((wide, SUB, LANE), f32),
             pltpu.VMEM((3,) + plane, f32),
-            pltpu.VMEM((2,) + plane, f32),
+            pltpu.VMEM((2, wide, SUB, LANE), f32),
             pltpu.VMEM((2,) + plane, f32),
             pltpu.VMEM((6,) + plane, f32),
-            pltpu.VMEM((STAGES, 2, PACK, SUB, LANE), f32),
-            pltpu.VMEM((STAGES, 2, PACK, SUB, LANE), f32),
-            pltpu.VMEM((STAGES, 16, LANE), f32),
-            pltpu.VMEM((STAGES, tiles, 16, LANE), f32),
+            pltpu.VMEM((2, 3, EXTRA[0], SUB, LANE), f32),
+            pltpu.VMEM((STAGES, FOLD, LANE), f32),
+            pltpu.VMEM((STAGES, tiles, FOLD, LANE), f32),
             pltpu.VMEM((rows, 2, SUB, LANE), f32),
             pltpu.VMEM((rows, 2, SUB, LANE), f32),
-            pltpu.SemaphoreType.DMA((STAGES, 2)),
-            pltpu.SemaphoreType.DMA((STAGES, 2)),
+            pltpu.SemaphoreType.DMA((3,)),
+            pltpu.SemaphoreType.DMA((3, 2)),
+            pltpu.SemaphoreType.DMA((3, 2)),
             pltpu.SemaphoreType.DMA((STAGES, tiles)),
             pltpu.SemaphoreType.DMA((STAGES, tiles)),
             pltpu.SemaphoreType.DMA((chunks,)),

time: 52.9 us -> 44.8 us (0.85)
  Pallas kernels: 49.4 us -> 41.4 us
    pallas_call x1, Pallas kernels: 49.4 us -> 41.4 us  [local(): pl.pallas_call(functools.partial(kernel, tiles, slices, rows), out_shape=...]
where the time goes in v2:
time: 44.8 us; the launch traced here: 44.6 us
  Pallas kernels  41.4 us (92%)
  local copies, waits for them, and re-layouts  3.24 us (7%)
    pallas_call x1, Pallas kernels, local(): pl.pallas_call(functools.partial(kernel, tiles, slices, rows), out_shape=...  41.4 us
    unnamed x7, local copies, waits for them, and re-layouts  3.24 us

profile of v2, /device:TPU:3, one launch (start us, length us, event | category | flops | bytes accessed | tf_op | source)
XLA Modules:
  0.0 44.6 jit_solution(492847520045554906)
XLA Ops:
  0.0 0.0 copy-start
  0.0 0.9 %copy-done = f32[1,2,16,1024]{3,2,1,0:T(8,128)S(1)} copy-done((f32[1,2,16,1024]{3,2,1,0:T(8,128)S(1)}, f32[1,2,16,1024]{3,2,1,0:T(8,128)}, u32[]{:S(2)}) %copy-start) | copy-done | bytes 131096
  0.9 0.0 copy-start.1
  0.9 0.8 %copy-done.1 = f32[16,1024]{1,0:T(8,128)S(1)} copy-done((f32[16,1024]{1,0:T(8,128)S(1)}, f32[16,1024]{1,0:T(8,128)}, u32[]{:S(2)}) %copy-start.1) | copy-done | bytes 65560
  1.7 0.0 copy-start.2
  1.7 0.8 %copy-done.2 = f32[16,1024]{1,0:T(8,128)S(1)} copy-done((f32[16,1024]{1,0:T(8,128)S(1)}, f32[16,1024]{1,0:T(8,128)}, u32[]{:S(2)}) %copy-start.2) | copy-done | bytes 65560
  2.6 41.4 %wake_step.1 = f32[1,2,16,1024]{3,2,1,0:T(8,128)S(1)} custom-call(f32[1,2,16,1024]{3,2,1,0:T(8,128)S(1)} %copy-done, f32[16,1024]{1,0:T(8,128)S(1)} %copy-done.1, f32[16,1024]{1,0:T(8,128)S(1)} %copy-done.2), custom_call_target="tpu_custom_call" | custom-call | tf_op jit(solution)/shard_map/wake_step/pallas_call | solution.py:407
  44.0 0.7 %copy.5 = f32[1,2,16,1024]{3,2,1,0:T(8,128)} copy(f32[1,2,16,1024]{3,2,1,0:T(8,128)S(1)} %wake_step.1) | data formatting | bytes 262144
Async XLA Ops:
  0.0 0.9 %copy-start = (f32[1,2,16,1024]{3,2,1,0:T(8,128)S(1)}, f32[1,2,16,1024]{3,2,1,0:T(8,128)}, u32[]{:S(2)}) copy-start(f32[1,2,16,1024]{3,2,1,0:T(8,128)} %state_ref.1) | copy-start | bytes 393220
  0.9 0.8 %copy-start.1 = (f32[16,1024]{1,0:T(8,128)S(1)}, f32[16,1024]{1,0:T(8,128)}, u32[]{:S(2)}) copy-start(f32[16,1024]{1,0:T(8,128)} %depth_ref.1) | copy-start | bytes 196612
  1.7 0.8 %copy-start.2 = (f32[16,1024]{1,0:T(8,128)S(1)}, f32[16,1024]{1,0:T(8,128)}, u32[]{:S(2)}) copy-start(f32[16,1024]{1,0:T(8,128)} %press_ref.1) | copy-start | bytes 196612

commit v3 on v2

--- a/solution.py
+++ b/solution.py
@@ -179,12 +179,6 @@
             dm[m, a:b] = inverse if inside is None else jnp.where(inside, inverse, 0.0)
         wfac[a:b] = (0.5 * LEVELS) / safe
 
-    pl.semaphore_wait(
-        barrier, tiles - 1 + has_prev.astype(jnp.int32) + has_next.astype(jnp.int32)
-    )
-    for k in range(3):
-        halo_both(k, start)
-
     columns(WIDE, end, None)
     own = x[1, WIDE:end]
     stiff = jnp.tanh(own)
@@ -196,6 +190,12 @@
     coarse[0] = cosine
     coarse[1] = stiff * sine
     coarse[2] = -sine
+
+    pl.semaphore_wait(
+        barrier, tiles - 1 + has_prev.astype(jnp.int32) + has_next.astype(jnp.int32)
+    )
+    for k in range(3):
+        halo_both(k, start)
 
     halo_both(0, arrive)
     columns(WIDE - 3, WIDE, has_lo)

time: 44.8 us -> 44.8 us (level)
  no operation moved by 1% of the time
where the time goes in v3:
time: 44.8 us; the launch traced here: 44.6 us
  Pallas kernels  41.4 us (92%)
  local copies, waits for them, and re-layouts  3.24 us (7%)
    pallas_call x1, Pallas kernels, local(): pl.pallas_call(functools.partial(kernel, tiles, slices, rows), out_shape=...  41.4 us
    unnamed x7, local copies, waits for them, and re-layouts  3.24 us

profile of v3, /device:TPU:3, one launch (start us, length us, event | category | flops | bytes accessed | tf_op | source)
XLA Modules:
  0.0 44.6 jit_solution(4129686915582529605)
XLA Ops:
  0.0 0.0 copy-start
  0.0 0.9 %copy-done = f32[1,2,16,1024]{3,2,1,0:T(8,128)S(1)} copy-done((f32[1,2,16,1024]{3,2,1,0:T(8,128)S(1)}, f32[1,2,16,1024]{3,2,1,0:T(8,128)}, u32[]{:S(2)}) %copy-start) | copy-done | bytes 131096
  0.9 0.0 copy-start.1
  0.9 0.8 %copy-done.1 = f32[16,1024]{1,0:T(8,128)S(1)} copy-done((f32[16,1024]{1,0:T(8,128)S(1)}, f32[16,1024]{1,0:T(8,128)}, u32[]{:S(2)}) %copy-start.1) | copy-done | bytes 65560
  1.7 0.0 copy-start.2
  1.7 0.8 %copy-done.2 = f32[16,1024]{1,0:T(8,128)S(1)} copy-done((f32[16,1024]{1,0:T(8,128)S(1)}, f32[16,1024]{1,0:T(8,128)}, u32[]{:S(2)}) %copy-start.2) | copy-done | bytes 65560
  2.6 41.4 %wake_step.1 = f32[1,2,16,1024]{3,2,1,0:T(8,128)S(1)} custom-call(f32[1,2,16,1024]{3,2,1,0:T(8,128)S(1)} %copy-done, f32[16,1024]{1,0:T(8,128)S(1)} %copy-done.1, f32[16,1024]{1,0:T(8,128)S(1)} %copy-done.2), custom_call_target="tpu_custom_call" | custom-call | tf_op jit(solution)/shard_map/wake_step/pallas_call | solution.py:407
  44.0 0.7 %copy.5 = f32[1,2,16,1024]{3,2,1,0:T(8,128)} copy(f32[1,2,16,1024]{3,2,1,0:T(8,128)S(1)} %wake_step.1) | data formatting | bytes 262144
Async XLA Ops:
  0.0 0.9 %copy-start = (f32[1,2,16,1024]{3,2,1,0:T(8,128)S(1)}, f32[1,2,16,1024]{3,2,1,0:T(8,128)}, u32[]{:S(2)}) copy-start(f32[1,2,16,1024]{3,2,1,0:T(8,128)} %state_ref.1) | copy-start | bytes 393220
  0.9 0.8 %copy-start.1 = (f32[16,1024]{1,0:T(8,128)S(1)}, f32[16,1024]{1,0:T(8,128)}, u32[]{:S(2)}) copy-start(f32[16,1024]{1,0:T(8,128)} %depth_ref.1) | copy-start | bytes 196612
  1.7 0.8 %copy-start.2 = (f32[16,1024]{1,0:T(8,128)S(1)}, f32[16,1024]{1,0:T(8,128)}, u32[]{:S(2)}) copy-start(f32[16,1024]{1,0:T(8,128)} %press_ref.1) | copy-start | bytes 196612
